TPU v7x, 32 devices: a whole 2x2x4 slice. The times are simulated.
32 devices in a mesh: seq: 8 (over z, core), batch: 4 (over y, x).
Axes of the slice: x: 2, y: 2, z: 4, core: 2. Of those that a mesh axis runs over, the one named last changes fastest.
Arguments:
- x_short: bfloat16 [8, 1024, 768], P('batch', 'seq'), may hold values from -6 to 6
- x_long: bfloat16 [8, 2048, 768], P('batch', 'seq'), may hold values from -6 to 6
- lengths: int32 [2, 8], P(None, 'batch'), may hold values from 256 to 2048, as said below
- cot_short: bfloat16 [8, 1024, 768], P('batch', 'seq'), may hold values from -6 to 6
- cot_long: bfloat16 [8, 2048, 768], P('batch', 'seq'), may hold values from -6 to 6
- w_qkv: bfloat16 [768, 2304], P(('seq', 'batch')), may hold values from -0.21875 to 0.21875
- w_out: bfloat16 [768, 768], P(('seq', 'batch')), may hold values from -1.25 to 1.25
- w_up: bfloat16 [768, 3072], P(('seq', 'batch')), may hold values from -0.21875 to 0.21875
- w_down: bfloat16 [3072, 768], P(('seq', 'batch')), may hold values from -0.109375 to 0.109375
- conv_kernel: bfloat16 [3, 2304], P(None, ('seq', 'batch')), may hold values from -3 to 3
- norm_params: bfloat16 [4, 768], P(None, ('seq', 'batch')), may hold values from -1.2 to 1.4
Outputs:
- y_short: bfloat16 [8, 1024, 768], P('batch', 'seq')
- y_long: bfloat16 [8, 2048, 768], P('batch', 'seq')
- dx_short: float32 [8, 1024, 768], P('batch', 'seq')
- dx_long: float32 [8, 2048, 768], P('batch', 'seq')
- grad_w_qkv: float32 [768, 2304], P(('seq', 'batch'))
- grad_w_out: float32 [768, 768], P(('seq', 'batch'))
- grad_w_up: float32 [768, 3072], P(('seq', 'batch'))
- grad_w_down: float32 [3072, 768], P(('seq', 'batch'))
- grad_conv_kernel: float32 [3, 2304], P(None, ('seq', 'batch'))
- grad_norm_params: float32 [4, 768], P(None, ('seq', 'batch'))
Inputs may be any that keep to these rules, and one draw needn't show every extreme that they name: Row 0 holds the lengths of the short sub-batch's sequences, the rest of each 1024-position slot being padding; row 1 those of the long sub-batch, in 2048-position slots. In each row, of the 2 sequences at one index of batch, one fills its whole slot and the other holds a quarter of its slot or more.
All inputs are finite; a program needn't handle non-finite values.
Results may differ from a plain program's by a relative error of at most 0.015.
The roundings to bfloat16 on the way count: a program that leaves them out, or rounds other values in their place, can miss the bound.
Values may be sent and summed in bfloat16 or wider, within the bound.
A program may use at most 320 MiB of HBM per device.

v0:
```python
import jax
import jax.numpy as jnp
from jax import lax
from jax.sharding import PartitionSpec as P

HEAD_DIM = 64


EPS = 1e-05
GROUP_HEADS = 2
NEG_FILL = -1e30


def from_behind(value, axis, by):
    count = lax.axis_size(axis)
    pairs = [(i, i + by) for i in range(count) if 0 <= i + by < count]
    return lax.ppermute(value, axis, pairs)


def layer_norm(values, gain, offset_term):
    average = jnp.mean(values, axis=-1, keepdims=True)
    centred = values - average
    inverse = lax.rsqrt(jnp.mean(centred * centred, axis=-1, keepdims=True) + EPS)
    normal = centred * inverse
    return (normal * gain + offset_term, normal, inverse)


def norm_back(grad, normal, inverse, gain):
    scaled_grad = grad * gain
    first_mean = jnp.mean(scaled_grad, axis=-1, keepdims=True)
    second_mean = jnp.mean(scaled_grad * normal, axis=-1, keepdims=True)
    return inverse * (scaled_grad - first_mean - normal * second_mean)


def front_part(inputs, full_weights):
    w_qkv = full_weights[0]
    kernel = full_weights[4].astype(jnp.float32)
    params = full_weights[5].astype(jnp.float32)
    saved = []
    tails = []
    for part_in in inputs:
        seq_count, block_rows, model_width = part_in.shape
        flat = part_in.reshape(seq_count * block_rows, model_width).astype(jnp.float32)
        normed, normal, inverse = layer_norm(flat, params[0], params[1])
        normed_low = normed.astype(jnp.bfloat16)
        projected = jnp.dot(normed_low, w_qkv, preferred_element_type=jnp.float32).astype(
            jnp.bfloat16
        )
        projected = projected.reshape(seq_count, block_rows, 3 * model_width)
        saved.append((flat, normal, inverse, normed_low, projected))
        tails.append(projected[:, block_rows - 2 :])
    received = from_behind((tails[0], tails[1]), "seq", 1)
    fronts = []
    for index_part in range(2):
        flat, normal, inverse, normed_low, projected = saved[index_part]
        block_rows = projected.shape[1]
        padded = jnp.concatenate([received[index_part], projected], axis=1).astype(jnp.float32)
        mixed = (
            kernel[0] * padded[:, 2:]
            + kernel[1] * padded[:, 1 : block_rows + 1]
            + kernel[2] * padded[:, :block_rows]
        )
        fronts.append((flat, normal, inverse, normed_low, padded, mixed.astype(jnp.bfloat16)))
    return fronts


def attend_block(queries, key_rows, value_rows, usable, grad_heads):
    scaling = queries.shape[-1] ** (-0.5)
    scores = jnp.einsum("sqhd,skhd->shqk", queries, key_rows, preferred_element_type=jnp.float32)
    masked = jnp.where(usable, scaling * scores, NEG_FILL)
    exp_terms = jnp.exp(masked - jnp.max(masked, axis=-1, keepdims=True))
    attn_probs = exp_terms / jnp.sum(exp_terms, axis=-1, keepdims=True)
    probs_low = attn_probs.astype(jnp.bfloat16)
    if grad_heads is None:
        attended = jnp.einsum(
            "shqk,skhd->sqhd", probs_low, value_rows, preferred_element_type=jnp.float32
        )
        return attended.astype(jnp.bfloat16)
    grad_probs = jnp.einsum(
        "sqhd,skhd->shqk", grad_heads, value_rows, preferred_element_type=jnp.float32
    )
    grad_values = jnp.einsum(
        "shqk,sqhd->skhd", probs_low, grad_heads, preferred_element_type=jnp.float32
    )
    row_delta = jnp.sum(attn_probs * grad_probs, axis=-1, keepdims=True)
    grad_scores = (scaling * attn_probs * (grad_probs - row_delta)).astype(jnp.bfloat16)
    grad_queries = jnp.einsum(
        "shqk,skhd->sqhd", grad_scores, key_rows, preferred_element_type=jnp.float32
    )
    grad_keys = jnp.einsum(
        "shqk,sqhd->skhd", grad_scores, queries, preferred_element_type=jnp.float32
    )
    return (grad_queries, grad_keys, grad_values)


def make_usable(query_pos, key_pos, seq_lengths):
    usable = (key_pos[None, None, :] <= query_pos[None, :, None]) & (
        key_pos[None, None, :] < seq_lengths[:, None, None]
    )
    return usable[:, None]


def attention(mixed, kv_full, seq_lengths, offset, grad_attended):
    seq_count, block_rows, three_width = mixed.shape
    model_width = three_width // 3
    full_len = kv_full.shape[1]
    queries = mixed[:, :, :model_width].reshape(seq_count, block_rows, -1, HEAD_DIM)
    key_rows = kv_full[:, :, :model_width].reshape(seq_count, full_len, -1, HEAD_DIM)
    value_rows = kv_full[:, :, model_width:].reshape(seq_count, full_len, -1, HEAD_DIM)
    positions = offset + jnp.arange(block_rows, dtype=jnp.int32)
    key_pos = jnp.arange(full_len, dtype=jnp.int32)
    usable = make_usable(positions, key_pos, seq_lengths)
    heads_total = queries.shape[2]
    grad_heads = None
    if grad_attended is not None:
        grad_heads = grad_attended.reshape(seq_count, block_rows, -1, HEAD_DIM)
    results = []
    for first_head in range(0, heads_total, GROUP_HEADS):
        last_head = first_head + GROUP_HEADS
        grad_part = None if grad_heads is None else grad_heads[:, :, first_head:last_head]
        results.append(
            attend_block(
                queries[:, :, first_head:last_head],
                key_rows[:, :, first_head:last_head],
                value_rows[:, :, first_head:last_head],
                usable,
                grad_part,
            )
        )
    if grad_heads is None:
        return jnp.concatenate(results, axis=2).reshape(seq_count, block_rows, model_width)
    grad_queries = jnp.concatenate([entry_set[0] for entry_set in results], axis=2).reshape(
        seq_count, block_rows, model_width
    )
    grad_keys = jnp.concatenate([entry_set[1] for entry_set in results], axis=2).reshape(
        seq_count, full_len, model_width
    )
    grad_values = jnp.concatenate([entry_set[2] for entry_set in results], axis=2).reshape(
        seq_count, full_len, model_width
    )
    return (grad_queries, grad_keys, grad_values)


def rest_part(front, kv_full, seq_lengths, offset, full_weights, cotangent_in):
    w_out, w_up, w_down = (full_weights[1], full_weights[2], full_weights[3])
    params = full_weights[5].astype(jnp.float32)
    flat, normal_one, inverse_one, normed_low, padded, mixed = front
    seq_count, block_rows, three_width = mixed.shape
    model_width = three_width // 3
    attended = attention(mixed, kv_full, seq_lengths, offset, None).reshape(
        seq_count * block_rows, model_width
    )
    middle = flat + jnp.dot(attended, w_out, preferred_element_type=jnp.float32)
    second, normal_two, inverse_two = layer_norm(middle, params[2], params[3])
    second_low = second.astype(jnp.bfloat16)
    upper = jnp.dot(second_low, w_up, preferred_element_type=jnp.float32)
    hidden = jnp.square(jnp.maximum(upper, 0.0)).astype(jnp.bfloat16)
    if cotangent_in is None:
        result_rows = middle + jnp.dot(hidden, w_down, preferred_element_type=jnp.float32)
        return result_rows.astype(jnp.bfloat16).reshape(seq_count, block_rows, model_width)
    cotangent = cotangent_in.reshape(seq_count * block_rows, model_width)
    grad_down = jnp.dot(hidden.T, cotangent, preferred_element_type=jnp.float32)
    grad_hidden = jnp.dot(cotangent, w_down.T, preferred_element_type=jnp.float32)
    grad_upper = (2.0 * jnp.maximum(upper, 0.0) * grad_hidden).astype(jnp.bfloat16)
    grad_up = jnp.dot(second_low.T, grad_upper, preferred_element_type=jnp.float32)
    grad_second = jnp.dot(grad_upper, w_up.T, preferred_element_type=jnp.float32)
    grad_middle = cotangent.astype(jnp.float32) + norm_back(
        grad_second, normal_two, inverse_two, params[2]
    )
    grad_middle_low = grad_middle.astype(jnp.bfloat16)
    grad_out = jnp.dot(attended.T, grad_middle_low, preferred_element_type=jnp.float32)
    grad_attended = jnp.dot(grad_middle_low, w_out.T, preferred_element_type=jnp.float32).astype(
        jnp.bfloat16
    )
    grad_attended = grad_attended.reshape(seq_count, block_rows, model_width)
    grad_queries, grad_keys, grad_values = attention(
        mixed, kv_full, seq_lengths, offset, grad_attended
    )
    key_term = jnp.concatenate([grad_keys, grad_values], axis=-1)
    norm_two = (jnp.sum(grad_second * normal_two, axis=0), jnp.sum(grad_second, axis=0))
    return (grad_queries, key_term, grad_middle, grad_out, grad_up, grad_down, norm_two)


def body(
    x_short,
    x_long,
    lengths,
    cot_short,
    cot_long,
    w_qkv,
    w_out,
    w_up,
    w_down,
    conv_kernel,
    norm_params,
):
    full_weights = (
        lax.all_gather(w_qkv, ("seq", "batch"), axis=0, tiled=True),
        lax.all_gather(w_out, ("seq", "batch"), axis=0, tiled=True),
        lax.all_gather(w_up, ("seq", "batch"), axis=0, tiled=True),
        lax.all_gather(w_down, ("seq", "batch"), axis=0, tiled=True),
        lax.all_gather(conv_kernel, ("seq", "batch"), axis=1, tiled=True),
        lax.all_gather(norm_params, ("seq", "batch"), axis=1, tiled=True),
    )
    inputs = (x_short, x_long)
    cotangents = (cot_short, cot_long)
    model_width = x_short.shape[2]
    offsets = (lax.axis_index("seq") * x_short.shape[1], lax.axis_index("seq") * x_long.shape[1])
    fronts = front_part(inputs, full_weights)
    kv_fwd = (
        lax.all_gather(fronts[0][5][:, :, model_width:], "seq", axis=1, tiled=True),
        lax.all_gather(fronts[1][5][:, :, model_width:], "seq", axis=1, tiled=True),
    )
    outputs = [
        rest_part(
            fronts[index_part],
            kv_fwd[index_part],
            lengths[index_part],
            offsets[index_part],
            full_weights,
            None,
        )
        for index_part in range(2)
    ]
    back_weights = (
        lax.all_gather(w_qkv, ("seq", "batch"), axis=0, tiled=True),
        lax.all_gather(w_out, ("seq", "batch"), axis=0, tiled=True),
        lax.all_gather(w_up, ("seq", "batch"), axis=0, tiled=True),
        lax.all_gather(w_down, ("seq", "batch"), axis=0, tiled=True),
        lax.all_gather(conv_kernel, ("seq", "batch"), axis=1, tiled=True),
        lax.all_gather(norm_params, ("seq", "batch"), axis=1, tiled=True),
    )
    fronts_back = front_part(inputs, back_weights)
    kv_back = (
        lax.all_gather(fronts_back[0][5][:, :, model_width:], "seq", axis=1, tiled=True),
        lax.all_gather(fronts_back[1][5][:, :, model_width:], "seq", axis=1, tiled=True),
    )
    partials = [
        rest_part(
            fronts_back[index_part],
            kv_back[index_part],
            lengths[index_part],
            offsets[index_part],
            back_weights,
            cotangents[index_part],
        )
        for index_part in range(2)
    ]
    kv_grads = (
        lax.psum_scatter(
            partials[0][1].astype(jnp.bfloat16), "seq", scatter_dimension=1, tiled=True
        ).astype(jnp.float32),
        lax.psum_scatter(
            partials[1][1].astype(jnp.bfloat16), "seq", scatter_dimension=1, tiled=True
        ).astype(jnp.float32),
    )
    grad_mixed = [
        jnp.concatenate([partials[index_part][0], kv_grads[index_part]], axis=-1)
        for index_part in range(2)
    ]
    received = (
        from_behind(grad_mixed[0][:, :2].astype(jnp.bfloat16), "seq", -1).astype(jnp.float32),
        from_behind(grad_mixed[1][:, :2].astype(jnp.bfloat16), "seq", -1).astype(jnp.float32),
    )
    kernel = back_weights[4].astype(jnp.float32)
    params = back_weights[5].astype(jnp.float32)
    w_qkv_full = back_weights[0]
    grad_qkv = jnp.zeros(w_qkv_full.shape, jnp.float32)
    grad_kernel = jnp.zeros(kernel.shape, jnp.float32)
    grad_norm = jnp.zeros((4, model_width), jnp.float32)
    grad_out = partials[0][3] + partials[1][3]
    grad_up = partials[0][4] + partials[1][4]
    grad_down = partials[0][5] + partials[1][5]
    input_grads = []
    for index_part in range(2):
        flat, normal_one, inverse_one, normed_low, padded, mixed = fronts_back[index_part]
        seq_count, block_rows, three_width = mixed.shape
        mixed_grad = grad_mixed[index_part]
        extended = jnp.concatenate([mixed_grad, received[index_part]], axis=1)
        grad_projected = (
            kernel[0] * extended[:, :block_rows]
            + kernel[1] * extended[:, 1 : block_rows + 1]
            + kernel[2] * extended[:, 2:]
        ).astype(jnp.bfloat16)
        grad_kernel = grad_kernel + jnp.stack(
            [
                jnp.sum(mixed_grad * padded[:, 2:], axis=(0, 1)),
                jnp.sum(mixed_grad * padded[:, 1 : block_rows + 1], axis=(0, 1)),
                jnp.sum(mixed_grad * padded[:, :block_rows], axis=(0, 1)),
            ]
        )
        grad_flat = grad_projected.reshape(seq_count * block_rows, three_width)
        grad_qkv = grad_qkv + jnp.dot(normed_low.T, grad_flat, preferred_element_type=jnp.float32)
        grad_normed = jnp.dot(grad_flat, w_qkv_full.T, preferred_element_type=jnp.float32)
        grad_input = partials[index_part][2] + norm_back(
            grad_normed, normal_one, inverse_one, params[0]
        )
        input_grads.append(grad_input.reshape(seq_count, block_rows, model_width))
        norm_two = partials[index_part][6]
        grad_norm = grad_norm + jnp.stack(
            [
                jnp.sum(grad_normed * normal_one, axis=0),
                jnp.sum(grad_normed, axis=0),
                norm_two[0],
                norm_two[1],
            ]
        )
    summed = (
        lax.psum_scatter(grad_qkv, ("seq", "batch"), scatter_dimension=0, tiled=True),
        lax.psum_scatter(grad_out, ("seq", "batch"), scatter_dimension=0, tiled=True),
        lax.psum_scatter(grad_up, ("seq", "batch"), scatter_dimension=0, tiled=True),
        lax.psum_scatter(grad_down, ("seq", "batch"), scatter_dimension=0, tiled=True),
        lax.psum_scatter(grad_kernel, ("seq", "batch"), scatter_dimension=1, tiled=True),
        lax.psum_scatter(grad_norm, ("seq", "batch"), scatter_dimension=1, tiled=True),
    )
    return (
        outputs[0],
        outputs[1],
        input_grads[0],
        input_grads[1],
        summed[0],
        summed[1],
        summed[2],
        summed[3],
        summed[4],
        summed[5],
    )


def solution(mesh):
    return jax.shard_map(
        body,
        mesh=mesh,
        in_specs=(
            P("batch", "seq", None),
            P("batch", "seq", None),
            P(None, "batch"),
            P("batch", "seq", None),
            P("batch", "seq", None),
            P(("seq", "batch"), None),
            P(("seq", "batch"), None),
            P(("seq", "batch"), None),
            P(("seq", "batch"), None),
            P(None, ("seq", "batch")),
            P(None, ("seq", "batch")),
        ),
        out_specs=(
            P("batch", "seq", None),
            P("batch", "seq", None),
            P("batch", "seq", None),
            P("batch", "seq", None),
            P(("seq", "batch"), None),
            P(("seq", "batch"), None),
            P(("seq", "batch"), None),
            P(("seq", "batch"), None),
            P(None, ("seq", "batch")),
            P(None, ("seq", "batch")),
        ),
        check_vma=False,
    )
```

profile of v0, /device:TPU:0, one launch (start us, length us, event | category | flops | bytes accessed | tf_op | source)
XLA Modules:
  0.0 1463.3 jit_solution(10304289859245028771)
XLA Ops:
  8.0 70.2 %all-gather = bf16[32,72,3]{1,2,0:T(4,128)(2,1)S(1)} all-gather(bf16[1,72,3]{1,2,0:T(4,128)(2,1)} %bitcast.553), channel_id=1, replica_groups=mesh['seq'=8,'batch'=4] {'seq','batch'}, dimensions={0}, use_global_device_ids=true | all-gather | bytes 14256 | tf_op jit(solution)/shard_map/all_gather | solution.py:202
  78.2 63.7 %all-gather.1 = bf16[32,24,4]{1,2,0:T(4,128)(2,1)S(1)} all-gather(bf16[1,24,4]{1,2,0:T(4,128)(2,1)} %bitcast.554), channel_id=1, replica_groups=mesh['seq'=8,'batch'=4] {'seq','batch'}, dimensions={0}, use_global_device_ids=true | all-gather | bytes 6336 | tf_op jit(solution)/shard_map/all_gather | solution.py:203
  176.6 41.3 %all-gather.11.cloned.1.call-done = bf16[2,1024,1536]{2,1,0:T(8,128)(2,1)} async-done(((bf16[2,128,1536]{2,1,0:T(8,128)(2,1)}), bf16[2,1024,1536]{2,1,0:T(8,128)(2,1)}) %all-gather.11.cloned.1.call-update) | async-done | bytes 6291472 | tf_op jit(solution)/shard_map/all_gather | solution.py:211
  285.3 53.6 %all-gather.15.cloned.1.call-done = bf16[768,3072]{1,0:T(8,128)(2,1)} async-done(((bf16[24,3072]{1,0:T(8,128)(2,1)}), bf16[768,3072]{1,0:T(8,128)(2,1)}) %all-gather.15.cloned.1.call-update) | async-done | bytes 4718608 | tf_op jit(solution)/shard_map/all_gather | solution.py:200
  343.0 61.1 %all-gather.17.cloned.1.call-done = bf16[3072,768]{1,0:T(8,128)(2,1)} async-done(((bf16[96,768]{1,0:T(8,128)(2,1)}), bf16[3072,768]{1,0:T(8,128)(2,1)}) %all-gather.17.cloned.1.call-update) | async-done | bytes 4718608 | tf_op jit(solution)/shard_map/all_gather | solution.py:201
  464.9 56.8 %all-gather.19.cloned.1.call-done = bf16[2,2048,1536]{2,1,0:T(8,128)(2,1)} async-done(((bf16[2,256,1536]{2,1,0:T(8,128)(2,1)}), bf16[2,2048,1536]{2,1,0:T(8,128)(2,1)}) %all-gather.19.cloned.1.call-update) | async-done | bytes 12582928 | tf_op jit(solution)/shard_map/all_gather | solution.py:212
  521.7 10.3 fusion.371
  532.0 8.8 copy.120
  569.6 9.2 copy.118
  578.9 9.6 fusion.387
  588.5 15.7 %fusion.386 = (f32[2,2,256]{2,1,0:T(2,128)S(1)}, f32[2,2,256,2048]{3,2,1,0:T(8,128)}) fusion(f32[2,2,256,2048]{3,2,1,0:T(8,128)} %fusion.226, pred[2,256,2048]{2,1,0:T(8,128)(4,1)S(1)} %copy-done.86), kind=kOutput, calls=%fused_computation.557 | output fusion | flops 12584959 | bytes 17829888 | tf_op jit(solution)/shard_map/sub | solution.py:71
  604.1 12.6 fusion.385
  616.8 12.8 fusion.384
  629.5 12.6 fusion.383
  642.1 12.6 fusion.382
  737.7 8.6 copy.140
  798.0 8.7 copy.139
  806.7 10.4 pad_maximum_fusion
  885.1 59.8 %reduce-scatter.11.cloned.1.call-done = bf16[2,256,1536]{2,1,0:T(8,128)(2,1)} async-done(((bf16[2,2048,1536]{2,1,0:T(8,128)(2,1)}), bf16[2,256,1536]{2,1,0:T(8,128)(2,1)}) %reduce-scatter.11.cloned.1.call-update) | async-done | bytes 1572880 | tf_op jit(solution)/shard_map/reduce_scatter | solution.py:253
  986.1 39.8 %all-reduce.2 = (f32[3,2304]{1,0:T(4,128)S(1)}, f32[4,768]{1,0:T(4,128)S(1)}) all-reduce(f32[3,2304]{1,0:T(4,128)S(1)} %maximum_add_fusion, f32[4,768]{1,0:T(4,128)S(1)} %maximum_add_fusion.1), channel_id=8, replica_groups=mesh['seq'=8,'batch'=4] {'seq','batch'}, use_global_device_ids=true, to_apply=%region_64.65.clone | all-reduce | flops 9984 | bytes 79872
  1030.2 17.7 %reduce-scatter.15.cloned.1.call-done = f32[24,768]{1,0:T(8,128)} async-done(((f32[768,768]{1,0:T(8,128)}), f32[24,768]{1,0:T(8,128)}) %reduce-scatter.15.cloned.1.call-update) | async-done | bytes 73744 | tf_op jit(solution)/shard_map/reduce_scatter | solution.py:310
  1047.9 141.9 %reduce-scatter.19.cloned.1.call-done = f32[96,768]{1,0:T(8,128)} async-done(((f32[3072,768]{1,0:T(8,128)}), f32[96,768]{1,0:T(8,128)}) %reduce-scatter.19.cloned.1.call-update) | async-done | bytes 294928 | tf_op jit(solution)/shard_map/reduce_scatter | solution.py:312
  1189.8 141.1 %reduce-scatter.17.cloned.1.call-done = f32[24,3072]{1,0:T(8,128)} async-done(((f32[768,3072]{1,0:T(8,128)}), f32[24,3072]{1,0:T(8,128)}) %reduce-scatter.17.cloned.1.call-update) | async-done | bytes 294928 | tf_op jit(solution)/shard_map/reduce_scatter | solution.py:311
  1330.9 125.4 %reduce-scatter.13.cloned.1.call-done = f32[24,2304]{1,0:T(8,128)} async-done(((f32[768,2304]{1,0:T(8,128)}), f32[24,2304]{1,0:T(8,128)}) %reduce-scatter.13.cloned.1.call-update) | async-done | bytes 221200 | tf_op jit(solution)/shard_map/reduce_scatter | solution.py:309
  (660 shorter events, 442.1 us)
Async XLA Ops:
  7.2 139.9 %all-gather.9.cloned.1.call-start = ((), (), s32[]{:S(2)}) async-start(), calls=%async_computation.6 | async-start | bytes 3649536 | tf_op jit(solution)/shard_map/all_gather | solution.py:198
  7.9 210.0 %all-gather.11.cloned.1.call-start = ((), (), s32[]{:S(2)}) async-start(), calls=%async_computation.7 | async-start | bytes 7077888 | tf_op jit(solution)/shard_map/all_gather | solution.py:211
  142.8 267.6 %copy-start.100 = (f32[768]{0:T(1024)}, f32[768]{0:T(1024)S(1)}, u32[]{:S(2)}) copy-start(f32[768]{0:T(1024)S(1)} %get-tuple-element.35) | copy-start | bytes 9220
  150.3 2.1 collective-permute-start
  155.1 127.1 %all-gather.13.cloned.1.call-start = ((), (), s32[]{:S(2)}) async-start(), calls=%async_computation.8 | async-start | bytes 1216512 | tf_op jit(solution)/shard_map/all_gather | solution.py:199
  155.8 183.2 %all-gather.15.cloned.1.call-start = ((), (), s32[]{:S(2)}) async-start(), calls=%async_computation.9 | async-start | bytes 4866048 | tf_op jit(solution)/shard_map/all_gather | solution.py:200
  156.4 247.7 %all-gather.17.cloned.1.call-start = ((), (), s32[]{:S(2)}) async-start(), calls=%async_computation.10 | async-start | bytes 4866048 | tf_op jit(solution)/shard_map/all_gather | solution.py:201
  157.0 364.7 %all-gather.19.cloned.1.call-start = ((), (), s32[]{:S(2)}) async-start(), calls=%async_computation.11 | async-start | bytes 14155776 | tf_op jit(solution)/shard_map/all_gather | solution.py:212
  162.9 3.2 collective-permute-start.1
  170.2 700.8 %reduce-scatter.9.cloned.1.call-start = ((), (), s32[]{:S(2)}) async-start(), calls=%async_computation.12 | async-start | bytes 7077888 | tf_op jit(solution)/shard_map/reduce_scatter | solution.py:250
  281.7 57.2 %copy-start.103 = (f32[768]{0:T(1024)S(1)}, f32[768]{0:T(1024)}, u32[]{:S(2)}) copy-start(f32[768]{0:T(1024)} %get-tuple-element.36) | copy-start | bytes 9220
  282.2 56.8 %copy-start.76 = (bf16[2,128,12,64]{1,0,3,2:T(2,128)(2,1)}, bf16[2,128,12,64]{1,0,3,2:T(2,128)(2,1)S(1)}, u32[]{:S(2)}) copy-start(bf16[2,128,12,64]{1,0,3,2:T(2,128)(2,1)S(1)} %copy.117) | copy-start | bytes 1179652
  284.2 126.2 %copy-start.113 = (f32[256]{0:T(256)}, f32[256]{0:T(256)S(1)}, u32[]{:S(2)}) copy-start(f32[256]{0:T(256)S(1)} %broadcast_multiply_fusion.10) | copy-start | bytes 3076
  285.3 125.1 %copy-start.124 = (f32[256]{0:T(256)}, f32[256]{0:T(256)S(1)}, u32[]{:S(2)}) copy-start(f32[256]{0:T(256)S(1)} %add_rsqrt_fusion.2) | copy-start | bytes 3076
  343.0 65.1 %copy-start.18 = (f32[256,3072]{1,0:T(8,128)}, f32[256,3072]{1,0:T(8,128)S(1)}, u32[]{:S(2)}) copy-start(f32[256,3072]{1,0:T(8,128)S(1)} %convolution_maximum_fusion) | copy-start | bytes 9437188
  464.9 480.0 %reduce-scatter.11.cloned.1.call-start = ((), (), s32[]{:S(2)}) async-start(), calls=%async_computation.13 | async-start | bytes 14155776 | tf_op jit(solution)/shard_map/reduce_scatter | solution.py:253
  588.5 85.1 %copy-start.52 = (f32[2,2,256,2048]{3,2,1,0:T(8,128)}, f32[2,2,256,2048]{3,2,1,0:T(8,128)S(1)}, u32[]{:S(2)}) copy-start(f32[2,2,256,2048]{3,2,1,0:T(8,128)S(1)} %get-tuple-element.94) | copy-start | bytes 25165828
  817.1 230.8 %reduce-scatter.15.cloned.1.call-start = ((), (), s32[]{:S(2)}) async-start(), calls=%async_computation.15 | async-start | bytes 2433024 | tf_op jit(solution)/shard_map/reduce_scatter | solution.py:310
  821.3 368.5 %reduce-scatter.19.cloned.1.call-start = ((), (), s32[]{:S(2)}) async-start(), calls=%async_computation.17 | async-start | bytes 9732096 | tf_op jit(solution)/shard_map/reduce_scatter | solution.py:312
  832.2 498.7 %reduce-scatter.17.cloned.1.call-start = ((), (), s32[]{:S(2)}) async-start(), calls=%async_computation.16 | async-start | bytes 9732096 | tf_op jit(solution)/shard_map/reduce_scatter | solution.py:311
  843.9 612.4 %reduce-scatter.13.cloned.1.call-start = ((), (), s32[]{:S(2)}) async-start(), calls=%async_computation.14 | async-start | bytes 7299072 | tf_op jit(solution)/shard_map/reduce_scatter | solution.py:309
  873.3 6.6 collective-permute-start.2
  879.8 66.8 %copy-start.24 = (f32[2,256,768]{2,1,0:T(8,128)}, f32[2,256,768]{2,1,0:T(8,128)S(1)}, u32[]{:S(2)}) copy-start(f32[2,256,768]{2,1,0:T(8,128)S(1)} %copy.141) | copy-start | bytes 4718596
  946.7 3.2 collective-permute-start.3
  (187 other events, 900.8 us)
Sparse Core Ops, SparseCore 0:
  10.9 62.9 all-gather.8
  155.2 62.7 all-gather.10
  220.9 52.7 all-gather.12
  276.4 62.5 all-gather.14
  341.7 62.3 all-gather.16
  406.1 115.5 all-gather.18
  524.0 67.9 reduce-scatter.8
  817.2 127.5 reduce-scatter.10
  950.7 97.1 reduce-scatter.14
  1055.2 134.5 reduce-scatter.18
  1196.3 134.5 reduce-scatter.16
  1337.9 118.2 reduce-scatter.12
where the time goes:
time: 1470 us; the launch traced here: 1460 us
  waiting for transfers between devices  703 us (48%)
  matrix products  268 us (18%)
  blocking collectives  174 us (12%)
  other arithmetic  166 us (11%)
  local copies, waits for them, and re-layouts  128 us (9%)
  between operations  17 us (1%)
    reduce_scatter x1, waiting for transfers between devices, body(): lax.psum_scatter(grad_down, ('seq', 'batch'), scatter_dimension=0, tiled=...  142 us
    reduce_scatter x1, waiting for transfers between devices, body(): lax.psum_scatter(grad_up, ('seq', 'batch'), scatter_dimension=0, tiled=True)  141 us
    reduce_scatter x1, waiting for transfers between devices, body(): lax.psum_scatter(grad_qkv, ('seq', 'batch'), scatter_dimension=0, tiled=T...  125 us
    sub x12, other arithmetic, attend_block(): exp_terms = jnp.exp(masked - jnp.max(masked, axis=-1, keepdims=True))  93.9 us
    all_gather x1, blocking collectives, body(): lax.all_gather(conv_kernel, ('seq', 'batch'), axis=1, tiled=True)  70.2 us
    all_gather x1, blocking collectives, body(): lax.all_gather(norm_params, ('seq', 'batch'), axis=1, tiled=True)  63.7 us
    all_gather x1, waiting for transfers between devices, body(): lax.all_gather(w_down, ('seq', 'batch'), axis=0, tiled=True)  61.1 us
    reduce_scatter x1, waiting for transfers between devices, body(): lax.psum_scatter(partials[1][1].astype(jnp.bfloat16), 'seq', scatter_dime...  59.8 us
  transfers between devices with their start and end apart: 16, of which 12 were waited for; matrix products, arithmetic and copies ran while one was open for 35% of the time, Pallas kernels for 0%

commit v1 on v0

--- a/solution.py
+++ b/solution.py
@@ -1,14 +1,874 @@
 import jax
 import jax.numpy as jnp
 from jax import lax
+from jax.experimental import pallas as pl
+from jax.experimental.pallas import tpu as pltpu
 from jax.sharding import PartitionSpec as P
 
+EPS = 1e-05
+NEG_FILL = -1e30
 HEAD_DIM = 64
-
-
-EPS = 1e-05
+LANES = 128
+TILE = 256
+PAD = 16
+MESH = pl.DeviceIdType.MESH
+F32 = jnp.float32
+BF16 = jnp.bfloat16
+
+
+def dot_nn(left, right):
+    return lax.dot_general(left, right, (((1,), (0,)), ((), ())), preferred_element_type=F32)
+
+
+def dot_nt(left, right):
+    return lax.dot_general(left, right, (((1,), (1,)), ((), ())), preferred_element_type=F32)
+
+
+def dot_tn(left, right):
+    return lax.dot_general(left, right, (((0,), (0,)), ((), ())), preferred_element_type=F32)
+
+
+def params_of(limit=58, **more):
+    return pltpu.CompilerParams(vmem_limit_bytes=limit * 2**20, **more)
+
+
+def vmem():
+    return pl.BlockSpec(memory_space=pltpu.VMEM)
+
+
+def smem():
+    return pl.BlockSpec(memory_space=pltpu.SMEM)
+
+
+def hbm():
+    return pl.BlockSpec(memory_space=pl.ANY)
+
+
+def normalise(values):
+    average = jnp.mean(values, axis=-1, keepdims=True)
+    centred = values - average
+    inverse = lax.rsqrt(jnp.mean(centred * centred, axis=-1, keepdims=True) + EPS)
+    return centred * inverse, inverse
+
+
+def norm_back(grad, normal, inverse, gain):
+    scaled_grad = grad * gain
+    first_mean = jnp.mean(scaled_grad, axis=-1, keepdims=True)
+    second_mean = jnp.mean(scaled_grad * normal, axis=-1, keepdims=True)
+    return inverse * (scaled_grad - first_mean - normal * second_mean)
+
+
+def lane_iota(rows):
+    return lax.broadcasted_iota(jnp.int32, (rows, LANES), 1)
+
+
+def position():
+    index = lax.axis_index("seq")
+    return index, lax.axis_index("batch"), index // 2, index % 2
+
+
+def greet(others, count):
+    barrier = pltpu.get_barrier_semaphore()
+    for other in others:
+        pl.semaphore_signal(barrier, inc=1, device_id=other, device_id_type=MESH)
+    pl.semaphore_wait(barrier, count)
+
+
+def exchange_kernel(x_ref, o_ref, local_sem, send_sem, recv_sem):
+    index, batch, _, _ = position()
+    count = x_ref.shape[0]
+    others = [(lax.rem(index + step, count), batch) for step in range(1, count)]
+    greet(others, count - 1)
+    own = pltpu.make_async_copy(x_ref.at[index], o_ref.at[index], local_sem)
+    own.start()
+    copies = []
+    for step in range(1, count):
+        target = lax.rem(index + step, count)
+        copy = pltpu.make_async_remote_copy(
+            src_ref=x_ref.at[target],
+            dst_ref=o_ref.at[index],
+            send_sem=send_sem.at[target],
+            recv_sem=recv_sem.at[index],
+            device_id=(target, batch),
+            device_id_type=MESH,
+        )
+        copy.start()
+        copies.append(copy)
+    for step in range(1, count):
+        source = lax.rem(index + count - step, count)
+        pltpu.make_async_remote_copy(
+            src_ref=x_ref.at[source],
+            dst_ref=o_ref.at[source],
+            send_sem=send_sem.at[source],
+            recv_sem=recv_sem.at[source],
+            device_id=(source, batch),
+            device_id_type=MESH,
+        ).wait_recv()
+    for copy in copies:
+        copy.wait_send()
+    own.wait()
+
+
+def exchange(x, collective_id):
+    count = x.shape[0]
+    return pl.pallas_call(
+        exchange_kernel,
+        out_shape=jax.ShapeDtypeStruct(x.shape, x.dtype),
+        in_specs=[hbm()],
+        out_specs=hbm(),
+        scratch_shapes=[
+            pltpu.SemaphoreType.DMA,
+            pltpu.SemaphoreType.DMA((count,)),
+            pltpu.SemaphoreType.DMA((count,)),
+        ],
+        compiler_params=pltpu.CompilerParams(collective_id=collective_id, has_side_effects=True),
+    )(x)
+
+
+def roles():
+    index, batch, z, core = position()
+    half = index // 4
+    near = jnp.where(half == 0, z, 3 - z)
+    partner_z = jnp.where(half == 0, 1 - z, 5 - z)
+    far_z = 2 - half
+    return index, batch, z, core, half, near, partner_z, far_z
+
+
+def z_of(half, place):
+    return jnp.where(half == 0, place, 3 - place)
+
+
+def greet_roles():
+    index, batch, z, core, half, near, partner_z, far_z = roles()
+    barrier = pltpu.get_barrier_semaphore()
+    pl.semaphore_signal(barrier, inc=1, device_id=(z * 2 + 1 - core, batch), device_id_type=MESH)
+    pl.semaphore_signal(barrier, inc=1, device_id=(partner_z * 2 + core, batch), device_id_type=MESH)
+
+    @pl.when(near == 1)
+    def _():
+        for place in (2, 3):
+            other = (z_of(half, place) * 2 + core, batch)
+            pl.semaphore_signal(barrier, inc=1, device_id=other, device_id_type=MESH)
+
+    pl.semaphore_wait(barrier, 3)
+
+
+def gather_kernel(xs_ref, xl_ref, os_ref, ol_ref, own_sem, send_sem, recv_sem, sib_send, sib_recv):
+    index, batch, z, core, half, near, partner_z, far_z = roles()
+    greet_roles()
+    sibling = (z * 2 + 1 - core, batch)
+    partner = (partner_z * 2 + core, batch)
+    far = (far_z * 2 + core, batch)
+    started = []
+    for part, (x_ref, o_ref) in enumerate(((xs_ref, os_ref), (xl_ref, ol_ref))):
+        rows = x_ref.shape[1]
+
+        def place_of(device, o_ref=o_ref, rows=rows):
+            return o_ref.at[pl.ds(device * rows, rows)]
+
+        def send(src, dst, send_s, recv_s, device):
+            copy = pltpu.make_async_remote_copy(
+                src_ref=src, dst_ref=dst, send_sem=send_s, recv_sem=recv_s,
+                device_id=device, device_id_type=MESH,
+            )
+            copy.start()
+            started.append(copy)
+
+        send(x_ref.at[half], place_of(index), send_sem.at[part, 0], recv_sem.at[part, near], partner)
+        send(x_ref.at[1 - half], place_of(index), send_sem.at[part, 1], recv_sem.at[part, 3 - near], far)
+        send(x_ref.at[half], place_of(index), sib_send.at[part, 0], sib_recv.at[part, near], sibling)
+        own = pltpu.make_async_copy(x_ref.at[half], place_of(index), own_sem.at[part])
+        own.start()
+        started.append(own)
+    for part, (x_ref, o_ref) in enumerate(((xs_ref, os_ref), (xl_ref, ol_ref))):
+        rows = x_ref.shape[1]
+        for slot, place in enumerate((1 - near, 2, 3)):
+            device = z_of(half, place) * 2 + core
+            block = o_ref.at[pl.ds(device * rows, rows)]
+
+            def wait_for(sem, block=block, device=device):
+                pltpu.make_async_remote_copy(
+                    src_ref=block, dst_ref=block, send_sem=send_sem.at[part, 0], recv_sem=sem,
+                    device_id=(device, batch), device_id_type=MESH,
+                ).wait_recv()
+
+            wait_for(recv_sem.at[part, place])
+            if slot > 0:
+                onward = pltpu.make_async_remote_copy(
+                    src_ref=block, dst_ref=block, send_sem=send_sem.at[part, 1 + slot],
+                    recv_sem=recv_sem.at[part, place], device_id=partner, device_id_type=MESH,
+                )
+
+                @pl.when(near == 1)
+                def _(onward=onward):
+                    onward.start()
+            across = pltpu.make_async_remote_copy(
+                src_ref=block, dst_ref=block, send_sem=sib_send.at[part, 1 + slot],
+                recv_sem=sib_recv.at[part, place], device_id=sibling, device_id_type=MESH,
+            )
+            across.start()
+            started.append(across)
+    for part, (x_ref, o_ref) in enumerate(((xs_ref, os_ref), (xl_ref, ol_ref))):
+        rows = x_ref.shape[1]
+        for place in range(4):
+            device = z_of(half, place) * 2 + 1 - core
+            block = o_ref.at[pl.ds(device * rows, rows)]
+            pltpu.make_async_remote_copy(
+                src_ref=block, dst_ref=block, send_sem=sib_send.at[part, 0],
+                recv_sem=sib_recv.at[part, place], device_id=sibling, device_id_type=MESH,
+            ).wait_recv()
+        own_place = o_ref.at[pl.ds(index * rows, rows)]
+        first, second, third, local = started[4 * part : 4 * part + 4]
+        first.wait_send()
+        second.wait_send()
+        third.wait_send()
+        local.wait()
+
+        @pl.when(near == 1)
+        def _(part=part, own_place=own_place):
+            for slot in (1, 2):
+                pltpu.make_async_remote_copy(
+                    src_ref=own_place, dst_ref=own_place, send_sem=send_sem.at[part, 1 + slot],
+                    recv_sem=recv_sem.at[part, 0], device_id=partner, device_id_type=MESH,
+                ).wait_send()
+    for copy in started[8:]:
+        copy.wait_send()
+
+
+def gather_rows(x_short, x_long, count):
+    width = x_short.shape[2]
+    return pl.pallas_call(
+        gather_kernel,
+        out_shape=(
+            jax.ShapeDtypeStruct((count * x_short.shape[1], width), x_short.dtype),
+            jax.ShapeDtypeStruct((count * x_long.shape[1], width), x_long.dtype),
+        ),
+        in_specs=[hbm(), hbm()],
+        out_specs=(hbm(), hbm()),
+        scratch_shapes=[
+            pltpu.SemaphoreType.DMA((2,)),
+            pltpu.SemaphoreType.DMA((2, 4)),
+            pltpu.SemaphoreType.DMA((2, 4)),
+            pltpu.SemaphoreType.DMA((2, 4)),
+            pltpu.SemaphoreType.DMA((2, 4)),
+        ],
+        compiler_params=pltpu.CompilerParams(collective_id=0, has_side_effects=True),
+    )(x_short, x_long)
+
+
+def sum_kernel(g_ref, o_ref, sib, total, got, sib_send, sib_recv, send_sem, recv_sem, own_sem):
+    index, batch, z, core, half, near, partner_z, far_z = roles()
+    greet_roles_sum()
+    sibling = (z * 2 + 1 - core, batch)
+    partner = (partner_z * 2 + core, batch)
+    order = (2, 3, 1, 0)
+
+    def copy_of(src, dst, send_s, recv_s, device):
+        return pltpu.make_async_remote_copy(
+            src_ref=src, dst_ref=dst, send_sem=send_s, recv_sem=recv_s,
+            device_id=device, device_id_type=MESH,
+        )
+
+    across = []
+    for place in order:
+        copy = copy_of(
+            g_ref.at[z_of(half, place) * 2 + 1 - core], sib.at[place],
+            sib_send.at[place], sib_recv.at[place], sibling,
+        )
+        copy.start()
+        across.append(copy)
+
+    def own_sum(place):
+        across[order.index(place)].wait_recv()
+        mine = g_ref[z_of(half, place) * 2 + core]
+        return mine.astype(F32) + sib[place].astype(F32)
+
+    @pl.when(near == 0)
+    def _():
+        out = []
+        for place in (2, 3, 1):
+            total[place] = own_sum(place).astype(BF16)
+            copy = copy_of(total.at[place], got.at[place], send_sem.at[place], recv_sem.at[place], partner)
+            copy.start()
+            out.append(copy)
+        mine = own_sum(0)
+        copy_of(total.at[0], got.at[0], send_sem.at[0], recv_sem.at[0], partner).wait_recv()
+        o_ref[half] = mine + got[0].astype(F32)
+        for copy in out:
+            copy.wait_send()
+
+    @pl.when(near == 1)
+    def _():
+        total[0] = own_sum(0).astype(BF16)
+        first = copy_of(total.at[0], got.at[0], send_sem.at[0], recv_sem.at[0], partner)
+        first.start()
+        out = [first]
+        for place in (2, 3):
+            mine = own_sum(place)
+            copy_of(total.at[place], got.at[place], send_sem.at[place], recv_sem.at[place], partner).wait_recv()
+            total[place] = (mine + got[place].astype(F32)).astype(BF16)
+            copy = copy_of(
+                total.at[place], got.at[4], send_sem.at[place], recv_sem.at[4],
+                (z_of(half, place) * 2 + core, batch),
+            )
+            copy.start()
+            out.append(copy)
+        mine = own_sum(1)
+        copy_of(total.at[1], got.at[1], send_sem.at[1], recv_sem.at[1], partner).wait_recv()
+        o_ref[half] = mine + got[1].astype(F32)
+        for copy in out:
+            copy.wait_send()
+
+    copy_of(total.at[0], got.at[4], send_sem.at[0], recv_sem.at[4], (far_z * 2 + core, batch)).wait_recv()
+    o_ref[1 - half] = got[4].astype(F32)
+    for copy in across:
+        copy.wait_send()
+
+
+def greet_roles_sum():
+    index, batch, z, core, half, near, partner_z, far_z = roles()
+    barrier = pltpu.get_barrier_semaphore()
+    pl.semaphore_signal(barrier, inc=1, device_id=(z * 2 + 1 - core, batch), device_id_type=MESH)
+    pl.semaphore_signal(barrier, inc=1, device_id=(partner_z * 2 + core, batch), device_id_type=MESH)
+    pl.semaphore_signal(barrier, inc=1, device_id=(far_z * 2 + core, batch), device_id_type=MESH)
+
+    @pl.when(near == 0)
+    def _():
+        pl.semaphore_wait(barrier, 2)
+
+    @pl.when(near == 1)
+    def _():
+        pl.semaphore_wait(barrier, 4)
+
+
+def sum_rows(grads):
+    count, rows, width = grads.shape
+    return pl.pallas_call(
+        sum_kernel,
+        out_shape=jax.ShapeDtypeStruct((2, rows, width), F32),
+        in_specs=[vmem()],
+        out_specs=vmem(),
+        scratch_shapes=[
+            pltpu.VMEM((4, rows, width), BF16),
+            pltpu.VMEM((4, rows, width), BF16),
+            pltpu.VMEM((5, rows, width), BF16),
+            pltpu.SemaphoreType.DMA((4,)),
+            pltpu.SemaphoreType.DMA((4,)),
+            pltpu.SemaphoreType.DMA((4,)),
+            pltpu.SemaphoreType.DMA((5,)),
+            pltpu.SemaphoreType.DMA,
+        ],
+        compiler_params=params_of(collective_id=3, has_side_effects=True),
+    )(grads)
+
+
+def shifted(window, by):
+    return pltpu.roll(window, by % window.shape[0], 0)
+
+
+def front_kernel(
+    lens_ref, xs_ref, xl_ref, wq_ref, ck_ref, np_ref,
+    osend, qa, ka, vb, kt, proj, normed, lse,
+    vt, ot,
+):
+    short_rows, long_rows = xs_ref.shape[0], xl_ref.shape[0]
+    width = xs_ref.shape[1]
+    parts = ((xs_ref, 0, PAD, short_rows), (xl_ref, short_rows, 2 * PAD + short_rows, long_rows))
+    gain, offset = np_ref[0:1], np_ref[1:2]
+    zeros = jnp.zeros((PAD, proj.shape[1]), BF16)
+    proj[0:PAD] = zeros
+    proj[PAD + short_rows : 2 * PAD + short_rows] = zeros
+    lanes = lane_iota(TILE)
+    low_half = lanes < HEAD_DIM
+    for part, (x_ref, base, pbase, total) in enumerate(parts):
+        length = lens_ref[part]
+
+        @pl.loop(0, total // TILE)
+        def _(step, x_ref=x_ref, base=base, pbase=pbase):
+            start = pl.multiple_of(step * TILE, TILE)
+            values = x_ref[pl.ds(start, TILE)].astype(F32)
+            normal, _ = normalise(values)
+            low = (normal * gain + offset).astype(BF16)
+            normed[pl.ds(pl.multiple_of(base + start, TILE), TILE)] = low
+            proj[pl.ds(pl.multiple_of(pbase + start, PAD), TILE)] = dot_nn(low, wq_ref[...]).astype(BF16)
+
+        @pl.loop(0, total // TILE)
+        def _(step, base=base, pbase=pbase, length=length):
+            start = pl.multiple_of(step * TILE, TILE)
+            window = proj[pl.ds(pl.multiple_of(pbase - PAD + start, PAD), TILE + PAD)].astype(F32)
+            mixed = (
+                ck_ref[0:1] * window[PAD:]
+                + ck_ref[1:2] * shifted(window, 1)[PAD:]
+                + ck_ref[2:3] * shifted(window, 2)[PAD:]
+            ).astype(BF16).astype(F32)
+            rows = pl.ds(pl.multiple_of(base + start, TILE), TILE)
+            q_pair, q_one = mixed[:, 0:128] * 0.125, mixed[:, 128:256] * 0.125
+            k_pair, k_one = mixed[:, 256:384], mixed[:, 384:512]
+            v_pair, v_one = mixed[:, 512:640], mixed[:, 640:768]
+            places = start + lax.broadcasted_iota(jnp.int32, (TILE, LANES), 0)
+            bias = jnp.where(places < length, 0.0, NEG_FILL)
+            at_zero = lanes == 0
+            at_half = lanes == HEAD_DIM
+            one_half = jnp.where(at_half, 1.0, 0.0)
+            one_zero = jnp.where(at_zero, 1.0, 0.0)
+            bias_half = jnp.where(at_half, bias, 0.0)
+            bias_zero = jnp.where(at_zero, bias, 0.0)
+            qa[0, rows] = jnp.where(low_half, q_pair, one_half).astype(BF16)
+            qa[1, rows] = jnp.where(low_half, one_zero, q_pair).astype(BF16)
+            qa[2, rows] = jnp.where(low_half, q_one, one_half).astype(BF16)
+            ka[0, rows] = jnp.where(low_half, k_pair, bias_half).astype(BF16)
+            ka[1, rows] = jnp.where(low_half, bias_zero, k_pair).astype(BF16)
+            ka[2, rows] = jnp.where(low_half, k_one, bias_half).astype(BF16)
+            vb[0, rows] = v_pair.astype(BF16)
+            vb[1, rows] = v_one.astype(BF16)
+            k_turned, k_turned_one = k_pair.T.astype(BF16), k_one.T.astype(BF16)
+            v_turned, v_turned_one = v_pair.T.astype(BF16), v_one.T.astype(BF16)
+            kt[0, :, rows] = k_turned[:HEAD_DIM]
+            kt[1, :, rows] = k_turned[HEAD_DIM:]
+            kt[2, :, rows] = k_turned_one[:HEAD_DIM]
+            vt[0, :, rows] = v_turned[:HEAD_DIM]
+            vt[1, :, rows] = v_turned[HEAD_DIM:]
+            vt[2, :, rows] = v_turned_one[:HEAD_DIM]
+
+    causal = lax.broadcasted_iota(jnp.int32, (TILE, TILE), 0) <= lax.broadcasted_iota(jnp.int32, (TILE, TILE), 1)
+
+    @pl.loop(0, 3)
+    def _(head):
+        for _, base, _, total in parts:
+            for block in range(total // TILE):
+                rows = slice(base + block * TILE, base + (block + 1) * TILE)
+                past = block * TILE
+                query = qa[head, rows]
+                diagonal = jnp.where(causal, dot_nt(ka[head, rows], query), NEG_FILL)
+                top = jnp.max(diagonal, axis=0, keepdims=True)
+                if past:
+                    before = dot_nt(ka[head, base : base + past], query)
+                    top = jnp.maximum(top, jnp.max(before, axis=0, keepdims=True))
+                    exp_before = jnp.exp(before - top)
+                exp_diagonal = jnp.exp(diagonal - top)
+                norm = jnp.sum(exp_diagonal, axis=0, keepdims=True)
+                if past:
+                    norm = norm + jnp.sum(exp_before, axis=0, keepdims=True)
+                lse[head, :, rows] = top + jnp.log(norm)
+                inverse = 1.0 / norm
+                result = dot_nn(vt[head, :, rows], (exp_diagonal * inverse).astype(BF16))
+                if past:
+                    result = result + dot_nn(
+                        vt[head, :, base : base + past], (exp_before * inverse).astype(BF16)
+                    )
+                ot[head, :, rows] = result
+
+    own_short, own_long = TILE // 2, TILE
+    for _, base, _, total in parts:
+        for block in range(total // TILE):
+            rows = slice(base + block * TILE, base + (block + 1) * TILE)
+            pair = jnp.concatenate([ot[0, :, rows], ot[1, :, rows]], axis=0).T.astype(BF16)
+            single = ot[2, :, rows]
+            if base:
+                osend[block, own_short : own_short + own_long] = pair
+                packed = jnp.concatenate([single[:, :LANES], single[:, LANES:]], axis=0).T
+                osend[block, own_short + own_long + own_short // 2 :] = packed.astype(BF16)
+            else:
+                turned = jnp.concatenate([single, single], axis=0).T
+                half = own_short // 2
+                for side in range(2):
+                    start = side * own_short
+                    osend[2 * block + side, 0:own_short] = pair[start : start + own_short]
+                    packed = jnp.where(
+                        lane_iota(half) < HEAD_DIM,
+                        turned[start : start + half],
+                        turned[start + half : start + own_short],
+                    )
+                    osend[2 * block + side, own_short + own_long : own_short + own_long + half] = packed.astype(BF16)
+
+
+def front(lens, xs, xl, wq, ck, norms, count):
+    short_rows, long_rows = xs.shape[0], xl.shape[0]
+    total = short_rows + long_rows
+    owned = total // count
+    out = jax.ShapeDtypeStruct
+    return pl.pallas_call(
+        front_kernel,
+        out_shape=(
+            out((count, owned * 3 // 2, LANES), BF16),
+            out((3, total, LANES), BF16),
+            out((3, total, LANES), BF16),
+            out((2, total, LANES), BF16),
+            out((3, HEAD_DIM, total), BF16),
+            out((total + 2 * PAD, 6 * LANES), BF16),
+            out((total, xs.shape[1]), BF16),
+            out((3, 1, total), F32),
+        ),
+        in_specs=[smem()] + [vmem()] * 5,
+        out_specs=tuple([vmem()] * 8),
+        scratch_shapes=[pltpu.VMEM((3, HEAD_DIM, total), BF16), pltpu.VMEM((3, HEAD_DIM, total), F32)],
+        compiler_params=params_of(),
+    )(lens, xs, xl, wq, ck, norms)
+
+
+def middle_kernel(
+    xs_ref, xl_ref, recv, cs_ref, cl_ref, wo_ref, wu_ref, wd_ref, np_ref,
+    ys_ref, yl_ref, gmid, gsend, gwo, gwu, gwd, gnorm,
+    att, middle, normal_two, inverse_two, second, second_t, cot, y_acc, gsec, gml,
+):
+    short, long = xs_ref.shape[1], xl_ref.shape[1]
+    owned = short + long
+    rows_all = 2 * owned
+    half = short // 2
+    lanes = lane_iota(owned // 2)
+    low_half = lanes < HEAD_DIM
+    for seq in range(2):
+        first = seq * owned
+        cot[first : first + short] = cs_ref[seq]
+        cot[first + short : first + owned] = cl_ref[seq]
+        for chip in range(2):
+            packs = []
+            for core in range(2):
+                source = recv.at[seq * 4 + chip * 2 + core]
+                block = 3 * chip + core
+                att[first : first + owned, block * LANES : (block + 1) * LANES] = source[0:owned]
+                packs.append(source[owned:].astype(F32))
+            swapped = [pltpu.roll(pack, HEAD_DIM, 1) for pack in packs]
+            early = jnp.where(low_half, packs[0], swapped[1]).astype(BF16)
+            late = jnp.where(low_half, swapped[0], packs[1]).astype(BF16)
+            columns = slice((3 * chip + 2) * LANES, (3 * chip + 3) * LANES)
+            att[first : first + half, columns] = early[:half]
+            att[first + half : first + short, columns] = late[:half]
+            att[first + short : first + short + long // 2, columns] = early[half:]
+            att[first + short + long // 2 : first + owned, columns] = late[half:]
+        middle[first : first + short] = xs_ref[seq].astype(F32)
+        middle[first + short : first + owned] = xl_ref[seq].astype(F32)
+
+    @pl.loop(0, rows_all // TILE)
+    def _(step):
+        rows = pl.ds(pl.multiple_of(step * TILE, TILE), TILE)
+        values = middle[rows] + dot_nn(att[rows], wo_ref[...])
+        middle[rows] = values
+        normal, inverse = normalise(values)
+        normal_two[rows] = normal
+        inverse_two[rows] = inverse
+        second[rows] = (normal * np_ref[2:3] + np_ref[3:4]).astype(BF16)
+        y_acc[rows] = values
+        gsec[rows] = jnp.zeros_like(values)
+
+    second_t[...] = second[...].T
+    inner = 512
+
+    @pl.loop(0, wu_ref.shape[1] // inner)
+    def _(step):
+        columns = pl.ds(pl.multiple_of(step * inner, inner), inner)
+        upper = jnp.maximum(dot_nn(second[...], wu_ref[:, columns]), 0.0)
+        hidden = (upper * upper).astype(BF16)
+        grad_hidden = dot_nt(cot[...], wd_ref[columns])
+        grad_upper = (2.0 * upper * grad_hidden).astype(BF16)
+        y_acc[...] += dot_nn(hidden, wd_ref[columns])
+        gwd[columns] = dot_tn(hidden, cot[...]).astype(BF16)
+        gwu[:, columns] = dot_nn(second_t[...], grad_upper).astype(BF16)
+        gsec[...] += dot_nt(grad_upper, wu_ref[:, columns])
+
+    gnorm[...] = jnp.zeros_like(gnorm)
+
+    @pl.loop(0, rows_all // TILE)
+    def _(step):
+        rows = pl.ds(pl.multiple_of(step * TILE, TILE), TILE)
+        grad = gsec[rows]
+        normal = normal_two[rows]
+        gnorm[0:1] += jnp.sum(grad * normal, axis=0, keepdims=True)
+        gnorm[1:2] += jnp.sum(grad, axis=0, keepdims=True)
+        total = cot[rows].astype(F32) + norm_back(grad, normal, inverse_two[rows], np_ref[2:3])
+        gmid[rows] = total
+        gml[rows] = total.astype(BF16)
+        second[rows] = dot_nt(gml[rows], wo_ref[...]).astype(BF16)
+
+    gwo[...] = dot_tn(att[...], gml[...]).astype(BF16)
+    for seq in range(2):
+        first = seq * owned
+        ys_ref[seq] = y_acc[first : first + short].astype(BF16)
+        yl_ref[seq] = y_acc[first + short : first + owned].astype(BF16)
+        for chip in range(2):
+            columns = slice((3 * chip + 2) * LANES, (3 * chip + 3) * LANES)
+            one = second[first : first + owned, columns].astype(F32)
+            early = jnp.concatenate([one[:half], one[short : short + long // 2]], axis=0)
+            late = jnp.concatenate([one[half:short], one[short + long // 2 :]], axis=0)
+            for core in range(2):
+                target = seq * 4 + chip * 2 + core
+                block = 3 * chip + core
+                gsend[target, 0:owned] = second[first : first + owned, block * LANES : (block + 1) * LANES]
+                if core == 0:
+                    packed = jnp.where(low_half, early, pltpu.roll(late, HEAD_DIM, 1))
+                else:
+                    packed = jnp.where(low_half, pltpu.roll(early, HEAD_DIM, 1), late)
+                gsend[target, owned:] = packed.astype(BF16)
+
+
+def middle_part(x_short, x_long, recv, cot_short, cot_long, w_out, w_up, w_down, norms):
+    width = x_short.shape[2]
+    rows = 2 * (x_short.shape[1] + x_long.shape[1])
+    out = jax.ShapeDtypeStruct
+    return pl.pallas_call(
+        middle_kernel,
+        out_shape=(
+            out(x_short.shape, BF16),
+            out(x_long.shape, BF16),
+            out((rows, width), F32),
+            out(recv.shape, BF16),
+            out(w_out.shape, BF16),
+            out(w_up.shape, BF16),
+            out(w_down.shape, BF16),
+            out((8, width), F32),
+        ),
+        in_specs=[vmem()] * 9,
+        out_specs=tuple([vmem()] * 8),
+        scratch_shapes=[
+            pltpu.VMEM((rows, width), BF16),
+            pltpu.VMEM((rows, width), F32),
+            pltpu.VMEM((rows, width), F32),
+            pltpu.VMEM((rows, 1), F32),
+            pltpu.VMEM((rows, width), BF16),
+            pltpu.VMEM((width, rows), BF16),
+            pltpu.VMEM((rows, width), BF16),
+            pltpu.VMEM((rows, width), F32),
+            pltpu.VMEM((rows, width), F32),
+            pltpu.VMEM((rows, width), BF16),
+        ],
+        compiler_params=params_of(),
+    )(x_short, x_long, recv, cot_short, cot_long, w_out, w_up, w_down, norms)
+
+
+def back_kernel(
+    xs_ref, xl_ref, normed, proj, qa, ka, vb, kt, lse, osend, grecv, wq_ref, ck_ref, np_ref,
+    gn_ref, gwq, gck, gnp,
+    do, delta, dqt, gm, gproj,
+):
+    short_rows, long_rows = xs_ref.shape[0], xl_ref.shape[0]
+    parts = (
+        (xs_ref, 0, PAD, 0, short_rows),
+        (xl_ref, short_rows, 2 * PAD + short_rows, PAD + short_rows, long_rows),
+    )
+    own_short, own_long = TILE // 2, TILE
+    owned = own_short + own_long
+    quarter = own_short // 2
+    gm[...] = jnp.zeros_like(gm)
+    gck[...] = jnp.zeros_like(gck)
+    gnp[...] = jnp.zeros_like(gnp)
+    pick = jnp.where(
+        (lax.broadcasted_iota(jnp.int32, (8, LANES), 1) < HEAD_DIM)
+        == (lax.broadcasted_iota(jnp.int32, (8, LANES), 0) == 0),
+        1.0,
+        0.0,
+    ).astype(F32)
+
+    def row_sums(product):
+        return lax.dot_general(
+            pick, product, (((1,), (1,)), ((), ())),
+            preferred_element_type=F32, precision=lax.Precision.HIGHEST,
+        )
+
+    def unpack(packed):
+        wide = packed.astype(F32)
+        return jnp.concatenate([wide, pltpu.roll(wide, HEAD_DIM, 1)], axis=0)
+
+    for part, (_, base, _, _, total) in enumerate(parts):
+        for block in range(total // TILE):
+            rows = slice(base + block * TILE, base + (block + 1) * TILE)
+            if part == 0:
+                grad_pair = jnp.concatenate([grecv[2 * block, 0:own_short], grecv[2 * block + 1, 0:own_short]], axis=0)
+                out_pair = jnp.concatenate([osend[2 * block, 0:own_short], osend[2 * block + 1, 0:own_short]], axis=0)
+                grad_one = jnp.concatenate(
+                    [unpack(grecv[2 * block + side, owned : owned + quarter]) for side in range(2)], axis=0
+                )
+                out_one = jnp.concatenate(
+                    [unpack(osend[2 * block + side, owned : owned + quarter]) for side in range(2)], axis=0
+                )
+            else:
+                grad_pair = grecv[block, own_short:owned]
+                out_pair = osend[block, own_short:owned]
+                grad_one = unpack(grecv[block, owned + quarter :])
+                out_one = unpack(osend[block, owned + quarter :])
+            low_half = lane_iota(TILE) < HEAD_DIM
+            grad_pair = grad_pair.astype(F32)
+            grad_one = jnp.where(low_half, grad_one, 0.0)
+            do[0, rows] = jnp.where(low_half, grad_pair, 0.0).astype(BF16)
+            do[1, rows] = jnp.where(low_half, 0.0, grad_pair).astype(BF16)
+            do[2, rows] = grad_one.astype(BF16)
+            sums = row_sums(grad_pair * out_pair.astype(F32))
+            delta[0, :, rows] = sums[0:1]
+            delta[1, :, rows] = sums[1:2]
+            delta[2, :, rows] = row_sums(grad_one * out_one)[0:1]
+
+    causal = lax.broadcasted_iota(jnp.int32, (TILE, TILE), 0) <= lax.broadcasted_iota(jnp.int32, (TILE, TILE), 1)
+
+    @pl.loop(0, 3)
+    def _(head):
+        pair = head // 2
+        own_lanes = (lane_iota(TILE) < HEAD_DIM) == (head != 1)
+        k_lanes = pl.ds(pl.multiple_of((2 + pair) * LANES, LANES), LANES)
+        v_lanes = pl.ds(pl.multiple_of((4 + pair) * LANES, LANES), LANES)
+        for _, base, _, gbase, total in parts:
+            for block in range(total // TILE):
+                rows = slice(base + block * TILE, base + (block + 1) * TILE)
+                query = qa[head, rows]
+                bare = jnp.where(own_lanes, query.astype(F32), 0.0).astype(BF16)
+                grad_out = do[head, rows]
+                stat, less = lse[head, :, rows], delta[head, :, rows]
+                spans = [(block * TILE, TILE, True)]
+                if block:
+                    spans.append((0, block * TILE, False))
+                grad_q = jnp.zeros((HEAD_DIM, TILE), F32)
+                for start, size, masked in spans:
+                    keys = slice(base + start, base + start + size)
+                    into = slice(gbase + start, gbase + start + size)
+                    scores = dot_nt(ka[head, keys], query)
+                    if masked:
+                        scores = jnp.where(causal, scores, NEG_FILL)
+                    probs = jnp.exp(scores - stat)
+                    grad_probs = dot_nt(vb[pair, keys], grad_out)
+                    gm[into, v_lanes] += dot_nn(probs.astype(BF16), grad_out)
+                    grad_scores = (probs * (grad_probs - less)).astype(BF16)
+                    gm[into, k_lanes] += dot_nn(grad_scores, bare)
+                    grad_q = grad_q + dot_nn(kt[head, :, keys], grad_scores)
+                dqt[head, :, rows] = 0.125 * grad_q
+
+    for _, base, _, gbase, total in parts:
+
+        @pl.loop(0, total // TILE)
+        def _(step, base=base, gbase=gbase):
+            start = pl.multiple_of(step * TILE, TILE)
+            rows = pl.ds(pl.multiple_of(base + start, TILE), TILE)
+            into = pl.ds(pl.multiple_of(gbase + start, PAD), TILE)
+            gm[into, 0:128] = jnp.concatenate([dqt[0, :, rows], dqt[1, :, rows]], axis=0).T
+            one = dqt[2, :, rows]
+            gm[into, 128:256] = jnp.concatenate([one, jnp.zeros_like(one)], axis=0).T
+
+    for part, (x_ref, base, pbase, gbase, total) in enumerate(parts):
+
+        @pl.loop(0, total // TILE)
+        def _(step, part=part, x_ref=x_ref, base=base, pbase=pbase, gbase=gbase):
+            start = pl.multiple_of(step * TILE, TILE)
+            rows = pl.ds(pl.multiple_of(base + start, TILE), TILE)
+            window = gm[pl.ds(pl.multiple_of(gbase + start, PAD), TILE + PAD)]
+            grad = window[:TILE]
+            projected_grad = (
+                ck_ref[0:1] * grad
+                + ck_ref[1:2] * shifted(window, -1)[:TILE]
+                + ck_ref[2:3] * shifted(window, -2)[:TILE]
+            ).astype(BF16)
+            gproj[rows] = projected_grad
+            past = proj[pl.ds(pl.multiple_of(pbase - PAD + start, PAD), TILE + PAD)].astype(F32)
+            gck[0:1] += jnp.sum(grad * past[PAD:], axis=0, keepdims=True)
+            gck[1:2] += jnp.sum(grad * shifted(past, 1)[PAD:], axis=0, keepdims=True)
+            gck[2:3] += jnp.sum(grad * shifted(past, 2)[PAD:], axis=0, keepdims=True)
+            grad_normed = dot_nt(projected_grad, wq_ref[...])
+            normal, _ = normalise(x_ref[pl.ds(start, TILE)].astype(F32))
+            gnp[0:1] += jnp.sum(grad_normed * normal, axis=0, keepdims=True)
+            gnp[1:2] += jnp.sum(grad_normed, axis=0, keepdims=True)
+            low = grad_normed.astype(BF16)
+            if part == 0:
+                gn_ref[2 * step, 0:own_short] = low[:own_short]
+                gn_ref[2 * step + 1, 0:own_short] = low[own_short:]
+            else:
+                gn_ref[step, own_short:] = low
+
+    for start in range(0, normed.shape[1], TILE):
+        gwq[start : start + TILE] = dot_tn(normed[:, start : start + TILE], gproj[...]).astype(BF16)
+
+
+def back_part(xs, xl, normed, proj, qa, ka, vb, kt, lse, osend, grecv, wq, ck, norms, count):
+    total = xs.shape[0] + xl.shape[0]
+    width = xs.shape[1]
+    out = jax.ShapeDtypeStruct
+    return pl.pallas_call(
+        back_kernel,
+        out_shape=(
+            out((count, total // count, width), BF16),
+            out(wq.shape, BF16),
+            out((8, wq.shape[1]), F32),
+            out((8, width), F32),
+        ),
+        in_specs=[vmem()] * 14,
+        out_specs=tuple([vmem()] * 4),
+        scratch_shapes=[
+            pltpu.VMEM((3, total, LANES), BF16),
+            pltpu.VMEM((3, 1, total), F32),
+            pltpu.VMEM((3, HEAD_DIM, total), F32),
+            pltpu.VMEM((total + 2 * PAD, 6 * LANES), F32),
+            pltpu.VMEM((total, 6 * LANES), BF16),
+        ],
+        compiler_params=params_of(),
+    )(xs, xl, normed, proj, qa, ka, vb, kt, lse, osend, grecv, wq, ck, norms)
+
+
+def take_columns(full, chip, core):
+    rows = full.shape[0]
+    blocks = full.reshape(rows, 3, 6, LANES)
+    pair = lax.dynamic_index_in_dim(blocks, 3 * chip + core, 2, keepdims=False)
+    shared = lax.dynamic_index_in_dim(blocks, 3 * chip + 2, 2, keepdims=False)
+    one = lax.dynamic_index_in_dim(shared.reshape(rows, 3, 2, HEAD_DIM), core, 2, keepdims=False)
+    one = jnp.concatenate([one, jnp.zeros_like(one)], axis=-1)
+    return jnp.stack([pair, one], axis=2).reshape(rows, 6 * LANES)
+
+
+def put_columns(group, chip, core):
+    rows = group.shape[0]
+    blocks = group.reshape(rows, 3, 2, LANES)
+    at = (lax.broadcasted_iota(jnp.int32, (1, 1, 6, 1), 2) == 3 * chip + core)
+    pairs = jnp.where(at, blocks[:, :, 0:1], 0)
+    one = blocks[:, :, 1:2, :HEAD_DIM]
+    zero = jnp.zeros_like(one)
+    shared = jnp.where(
+        core == 0, jnp.concatenate([one, zero], axis=-1), jnp.concatenate([zero, one], axis=-1)
+    )
+    at_one = (lax.broadcasted_iota(jnp.int32, (1, 1, 6, 1), 2) == 3 * chip + 2)
+    return (pairs + jnp.where(at_one, shared, 0)).reshape(rows, 18 * LANES).astype(group.dtype)
+
+
+def split_body(
+    x_short, x_long, lengths, cot_short, cot_long, w_qkv, w_out, w_up, w_down, conv_kernel, norm_params
+):
+    both = ("seq", "batch")
+    count = lax.axis_size("seq")
+    index = lax.axis_index("seq")
+    half, chip, core = index // 4, (index // 2) % 2, index % 2
+    full_qkv = lax.all_gather(w_qkv, both, axis=0, tiled=True)
+    kernel = lax.all_gather(conv_kernel, both, axis=1, tiled=True).astype(F32)
+    norms = lax.all_gather(norm_params, both, axis=1, tiled=True).astype(F32)
+    full_out = lax.all_gather(w_out, both, axis=0, tiled=True)
+    full_up = lax.all_gather(w_up, both, axis=0, tiled=True)
+    full_down = lax.all_gather(w_down, both, axis=0, tiled=True)
+    xs, xl = gather_rows(x_short, x_long, count)
+    wq = take_columns(full_qkv, chip, core)
+    ck = take_columns(kernel, chip, core)
+    lens = lax.dynamic_index_in_dim(lengths, half, 1, keepdims=False)
+    osend, qa, ka, vb, kt, proj, normed, lse = front(lens, xs, xl, wq, ck, norms, count)
+    recv = exchange(osend, 1)
+    y_short, y_long, gmid, gsend, gwo, gwu, gwd, gnorm = middle_part(
+        x_short, x_long, recv, cot_short, cot_long, full_out, full_up, full_down, norms
+    )
+    grecv = exchange(gsend, 2)
+    gn, gwq, gck, gnp = back_part(
+        xs, xl, normed, proj, qa, ka, vb, kt, lse, osend, grecv, wq, ck, norms, count
+    )
+    grad_normed = sum_rows(gn)
+    short = x_short.shape[1]
+    gmid = gmid.reshape(2, -1, gmid.shape[1])
+    dx = []
+    for x, rows in ((x_short, slice(0, short)), (x_long, slice(short, None))):
+        normal, inverse = normalise(x.astype(F32))
+        dx.append(gmid[:, rows] + norm_back(grad_normed[:, rows], normal, inverse, norms[0]))
+    scatter = lambda value, axis: lax.psum_scatter(value, both, scatter_dimension=axis, tiled=True)
+    grad_norm = jnp.concatenate([gnp[0:2], gnorm[0:2]], axis=0)
+    return (
+        y_short, y_long, dx[0], dx[1],
+        scatter(put_columns(gwq, chip, core), 0).astype(F32),
+        scatter(gwo, 0).astype(F32),
+        scatter(gwu, 0).astype(F32),
+        scatter(gwd, 0).astype(F32),
+        scatter(put_columns(gck[0:3], chip, core), 1),
+        scatter(grad_norm, 1),
+    )
+
+
 GROUP_HEADS = 2
-NEG_FILL = -1e30
 
 
 def from_behind(value, axis, by):
@@ -25,7 +885,7 @@
     return (normal * gain + offset_term, normal, inverse)
 
 
-def norm_back(grad, normal, inverse, gain):
+def norm_back_flat(grad, normal, inverse, gain):
     scaled_grad = grad * gain
     first_mean = jnp.mean(scaled_grad, axis=-1, keepdims=True)
     second_mean = jnp.mean(scaled_grad * normal, axis=-1, keepdims=True)
@@ -164,7 +1024,7 @@
     grad_upper = (2.0 * jnp.maximum(upper, 0.0) * grad_hidden).astype(jnp.bfloat16)
     grad_up = jnp.dot(second_low.T, grad_upper, preferred_element_type=jnp.float32)
     grad_second = jnp.dot(grad_upper, w_up.T, preferred_element_type=jnp.float32)
-    grad_middle = cotangent.astype(jnp.float32) + norm_back(
+    grad_middle = cotangent.astype(jnp.float32) + norm_back_flat(
         grad_second, normal_two, inverse_two, params[2]
     )
     grad_middle_low = grad_middle.astype(jnp.bfloat16)
@@ -181,7 +1041,7 @@
     return (grad_queries, key_term, grad_middle, grad_out, grad_up, grad_down, norm_two)
 
 
-def body(
+def general_body(
     x_short,
     x_long,
     lengths,
@@ -292,7 +1152,7 @@
         grad_flat = grad_projected.reshape(seq_count * block_rows, three_width)
         grad_qkv = grad_qkv + jnp.dot(normed_low.T, grad_flat, preferred_element_type=jnp.float32)
         grad_normed = jnp.dot(grad_flat, w_qkv_full.T, preferred_element_type=jnp.float32)
-        grad_input = partials[index_part][2] + norm_back(
+        grad_input = partials[index_part][2] + norm_back_flat(
             grad_normed, normal_one, inverse_one, params[0]
         )
         input_grads.append(grad_input.reshape(seq_count, block_rows, model_width))
@@ -328,8 +1188,9 @@
 
 
 def solution(mesh):
+    split = mesh.shape["seq"] == 8
     return jax.shard_map(
-        body,
+        split_body if split else general_body,
         mesh=mesh,
         in_specs=(
             P("batch", "seq", None),

time: 1470 us -> 776 us (0.53)
  waiting for transfers between devices: 703 us -> 211 us
  Pallas kernels: 0 us -> 319 us
  matrix products: 268 us -> 0 us
  other arithmetic: 166 us -> 17.1 us
  local copies, waits for them, and re-layouts: 128 us -> 30.9 us
    pallas_call x0 -> x7, Pallas kernels: none -> 319 us  [the longest x1 65.4 us: sum_rows(): pl.pallas_call(sum_kernel, out_shape=jax.ShapeDtypeStruct((2, rows, width...]
    reduce_scatter x6 -> x3, waiting for transfers between devices: 486 us -> 205 us  [split_body(): lax.psum_scatter(value, both, scatter_dimension=axis, tiled=True)]
    dot_general x96 -> x0, matrix products: 268 us -> none  [the longest x12 43 us: attend_block(): jnp.einsum('sqhd,skhd->shqk', grad_heads, value_rows, preferred_element_t...]
    all_gather x6 -> x4, waiting for transfers between devices: 213 us -> 2.28 us  [the longest x1 2.22 us: split_body(): full_down = lax.all_gather(w_down, both, axis=0, tiled=True)]
    sub x12 -> x0, other arithmetic: 93.9 us -> none  [attend_block(): exp_terms = jnp.exp(masked - jnp.max(masked, axis=-1, keepdims=True))]
    slice x18 -> x7, local copies, waits for them, and re-layouts: 50.6 us -> 4.65 us  [the longest x2 2.67 us: split_body(): grad_norm = jnp.concatenate([gnp[0:2], gnorm[0:2]], axis=0)]
    unnamed x395 -> x40, local copies, waits for them, and re-layouts: 45.7 us -> 9.36 us
    convert_element_type x23 -> x3, other arithmetic: 32.8 us -> 4.7 us  [the longest x1 1.64 us: split_body(): scatter(gwu, 0).astype(F32)]
  transfers between devices with their start and end apart: 16 -> 8, of which waited for: 12 -> 3; matrix products, arithmetic and copies ran while one was open for 35% -> 6% of each run, Pallas kernels for 0% -> 37%
where the time goes in v1:
time: 776 us; the launch traced here: 766 us
  Pallas kernels  319 us (41%)
  waiting for transfers between devices  211 us (27%)
  blocking collectives  173 us (22%)
  local copies, waits for them, and re-layouts  30.9 us (4%)
  other arithmetic  17.1 us (2%)
  between operations  14.9 us (2%)
    reduce_scatter x3, waiting for transfers between devices, split_body(): lax.psum_scatter(value, both, scatter_dimension=axis, tiled=True)  205 us
    all_gather x1, blocking collectives, split_body(): kernel = lax.all_gather(conv_kernel, both, axis=1, tiled=True).astype(F32)  70 us
    pallas_call x1, Pallas kernels, sum_rows(): pl.pallas_call(sum_kernel, out_shape=jax.ShapeDtypeStruct((2, rows, width...  65.4 us
    all_gather x1, blocking collectives, split_body(): norms = lax.all_gather(norm_params, both, axis=1, tiled=True).astype(F32)  63.7 us
    pallas_call x1, Pallas kernels, gather_rows(): pl.pallas_call(gather_kernel, out_shape=(jax.ShapeDtypeStruct((count * x_...  60.4 us
    pallas_call x1, Pallas kernels, back_part(): pl.pallas_call(back_kernel, out_shape=(out((count, total // count, width)...  58.1 us
    pallas_call x2, Pallas kernels, exchange(): pl.pallas_call(exchange_kernel, out_shape=jax.ShapeDtypeStruct(x.shape, x...  54.8 us
    pallas_call x1, Pallas kernels, front(): pl.pallas_call(front_kernel, out_shape=(out((count, owned * 3 // 2, LANES...  41.3 us
  transfers between devices with their start and end apart: 8, of which 3 were waited for; matrix products, arithmetic and copies ran while one was open for 6% of the time, Pallas kernels for 37%

profile of v1, /device:TPU:0, one launch (start us, length us, event | category | flops | bytes accessed | tf_op | source)
XLA Modules:
  0.0 766.0 jit_solution(1344384633303378542)
XLA Ops:
  10.1 70.0 %all-gather = bf16[32,72,3]{1,2,0:T(4,128)(2,1)S(1)} all-gather(bf16[1,72,3]{1,2,0:T(4,128)(2,1)} %bitcast.66), channel_id=1, replica_groups=mesh['seq'=8,'batch'=4] {'seq','batch'}, dimensions={0}, use_global_device_ids=true | all-gather | bytes 14256 | tf_op jit(solution)/shard_map/all_gather | solution.py:833
  81.1 63.7 %all-gather.1 = bf16[32,24,4]{1,2,0:T(4,128)(2,1)S(1)} all-gather(bf16[1,24,4]{1,2,0:T(4,128)(2,1)} %bitcast.67), channel_id=1, replica_groups=mesh['seq'=8,'batch'=4] {'seq','batch'}, dimensions={0}, use_global_device_ids=true | all-gather | bytes 6336 | tf_op jit(solution)/shard_map/all_gather | solution.py:834
  146.4 60.4 %shard_map.186 = (bf16[1024,768]{1,0:T(8,128)(2,1)}, bf16[2048,768]{1,0:T(8,128)(2,1)}) custom-call(bf16[2,128,768]{2,1,0:T(8,128)(2,1)} %xs_ref.3, bf16[2,256,768]{2,1,0:T(8,128)(2,1)} %xl_ref.3), custom_call_target="tpu_custom_call" | custom-call | tf_op jit(solution)/shard_map/pallas_call | solution.py:240
  206.8 4.5 copy.57
  211.6 1.5 copy.78.wq_ref
  213.1 41.3 %shard_map.187 = (bf16[8,576,128]{2,1,0:T(8,128)(2,1)}, bf16[3,3072,128]{2,1,0:T(8,128)(2,1)}, bf16[3,3072,128]{2,1,0:T(8,128)(2,1)}, bf16[2,3072,128]{2,1,0:T(8...) custom-call(s32[2]{0:T(128)} %fusion.21.lens_ref, ...), custom_call_target="tpu_custom_call" | custom-call | tf_op jit(solution)/shard_map/pallas_call | solution.py:490
  254.4 26.7 %shard_map.188.recv = bf16[8,576,128]{2,1,0:T(8,128)(2,1)} custom-call(bf16[8,576,128]{2,1,0:T(8,128)(2,1)} %get-tuple-element.34.x_ref.osend), custom_call_target="tpu_custom_call" | custom-call | tf_op jit(solution)/shard_map/pallas_call | solution.py:114
  281.2 2.2 all-gather.13.cloned.1.call-done.wd_ref
  283.4 38.9 %shard_map.189 = (bf16[2,128,768]{2,1,0:T(8,128)(2,1)}, bf16[2,256,768]{2,1,0:T(8,128)(2,1)}, f32[768,768]{1,0:T(8,128)}, bf16[8,576,128]{2,1,0:T(8,128)(2,1)}, ...) custom-call(bf16[2,128,768]{2,1,0:T(8,128)(2,1)} %xs_ref.3, ...), custom_call_target="tpu_custom_call" | custom-call | tf_op jit(solution)/shard_map/pallas_call | solution.py:608
  322.6 28.1 %shard_map.190.grecv = bf16[8,576,128]{2,1,0:T(8,128)(2,1)} custom-call(bf16[8,576,128]{2,1,0:T(8,128)(2,1)} %get-tuple-element.45.x_ref), custom_call_target="tpu_custom_call" | custom-call | tf_op jit(solution)/shard_map/pallas_call | solution.py:114
  350.7 58.1 %shard_map.191 = (bf16[8,384,768]{2,1,0:T(8,128)(2,1)}, bf16[768,768]{1,0:T(8,128)(2,1)}, f32[8,768]{1,0:T(8,128)}, f32[8,768]{1,0:T(8,128)}) custom-call(bf16[1024,768]{1,0:T(8,128)(2,1)} %get-tuple-element.32.xs_ref, bf16[2048,768]{1,0:T(8,128)(2,1)} %get-tuple-element.33.xl_ref, bf16[3072,768]{1,0:T(8,128)(2,1)} %get-tuple-element.38.normed, ...), custom_call_target="tpu_custom_call" | custom-call | tf_op jit(solution)/shard_map/pallas_call | solution.py:780
  408.9 2.7 reshape.121
  414.4 3.0 copy.85
  417.4 1.9 fusion
  419.3 4.0 copy.70
  432.2 65.4 %shard_map.192 = f32[2,384,768]{2,1,0:T(8,128)} custom-call(bf16[8,384,768]{2,1,0:T(8,128)(2,1)} %get-tuple-element.46.g_ref), custom_call_target="tpu_custom_call" | custom-call | tf_op jit(solution)/shard_map/pallas_call | solution.py:346
  498.8 38.8 %all-reduce.8 = (f32[3,2304]{1,0:T(4,128)}, f32[4,768]{1,0:T(4,128)}) all-reduce(f32[3,2304]{1,0:T(4,128)} %select_add_fusion, f32[4,768]{1,0:T(4,128)} %pad_maximum_fusion.1), channel_id=6, replica_groups=mesh['seq'=8,'batch'=4] {'seq','batch'}, use_global_device_ids=true, to_apply=%region_12.13.clone | all-reduce | flops 9984 | bytes 79872
  540.3 1.6 fusion.20
  542.0 2.1 fusion.10
  545.3 1.7 fusion.8
  550.6 94.2 %reduce-scatter.11.cloned.1.call-done = bf16[24,3072]{1,0:T(8,128)(2,1)} async-done(((bf16[768,3072]{1,0:T(8,128)(2,1)}), bf16[24,3072]{1,0:T(8,128)(2,1)}) %reduce-scatter.11.cloned.1.call-update) | async-done | bytes 147472 | tf_op jit(solution)/shard_map/reduce_scatter | solution.py:858
  644.8 1.6 convert_element_type.33
  646.4 110.8 %reduce-scatter.13.cloned.1.call-done = bf16[96,768]{1,0:T(8,128)(2,1)} async-done(((bf16[3072,768]{1,0:T(8,128)(2,1)}), bf16[96,768]{1,0:T(8,128)(2,1)}) %reduce-scatter.13.cloned.1.call-update) | async-done | bytes 147472 | tf_op jit(solution)/shard_map/reduce_scatter | solution.py:858
  757.3 1.6 convert_element_type.34
  (113 shorter events, 26.0 us)
Async XLA Ops:
  7.2 138.5 %copy-start = (s32[2,2]{1,0:T(2,128)S(1)}, s32[2,2]{1,0:T(2,128)}, u32[]{:S(2)}) copy-start(s32[2,2]{1,0:T(2,128)} %param.13) | copy-start | bytes 52
  7.2 199.6 %all-gather.7.cloned.1.call-start = ((), (), s32[]{:S(2)}) async-start(), calls=%async_computation.4 | async-start | bytes 3649536 | tf_op jit(solution)/shard_map/all_gather | solution.py:832
  7.9 273.2 %all-gather.9.cloned.1.call-start = ((), (), s32[]{:S(2)}) async-start(), calls=%async_computation.5 | async-start | bytes 1216512 | tf_op jit(solution)/shard_map/all_gather | solution.py:835
  8.7 272.5 %all-gather.11.cloned.1.call-start = ((), (), s32[]{:S(2)}) async-start(), calls=%async_computation.6 | async-start | bytes 4866048 | tf_op jit(solution)/shard_map/all_gather | solution.py:836
  9.4 274.0 %all-gather.13.cloned.1.call-start = ((), (), s32[]{:S(2)}) async-start(), calls=%async_computation.7 | async-start | bytes 4866048 | tf_op jit(solution)/shard_map/all_gather | solution.py:837
  10.0 537.0 %reduce-scatter.9.cloned.1.call-start = ((), (), s32[]{:S(2)}) async-start(), calls=%async_computation.8 | async-start | bytes 1216512 | tf_op jit(solution)/shard_map/reduce_scatter | solution.py:858
  322.3 226.1 %reduce-scatter.15.cloned.1.call-start = ((), (), s32[]{:S(2)}) async-start(), calls=%async_computation.11 | async-start | bytes 3649536
  423.3 221.5 %reduce-scatter.11.cloned.1.call-start = ((), (), s32[]{:S(2)}) async-start(), calls=%async_computation.9 | async-start | bytes 4866048 | tf_op jit(solution)/shard_map/reduce_scatter | solution.py:858
  424.1 333.2 %reduce-scatter.13.cloned.1.call-start = ((), (), s32[]{:S(2)}) async-start(), calls=%async_computation.10 | async-start | bytes 4866048 | tf_op jit(solution)/shard_map/reduce_scatter | solution.py:858
  424.1 1.4 copy-start.4
  424.1 2.2 copy-start.2
  424.8 3.2 copy-start.14
  425.7 0.6 copy-start.11
  432.1 65.4 %copy-start.8 = (f32[2,768]{1,0:T(2,128)S(1)}, f32[2,768]{1,0:T(2,128)}, u32[]{:S(2)}) copy-start(f32[2,768]{1,0:T(2,128)} %slice.47) | copy-start | bytes 18436
  432.1 65.4 %copy-start.9 = (f32[2,768]{1,0:T(2,128)S(1)}, f32[2,768]{1,0:T(2,128)}, u32[]{:S(2)}) copy-start(f32[2,768]{1,0:T(2,128)} %slice.48) | copy-start | bytes 18436
  432.1 66.0 %copy-start.6 = (f32[3,2304]{1,0:T(4,128)S(1)}, f32[3,2304]{1,0:T(4,128)}, u32[]{:S(2)}) copy-start(f32[3,2304]{1,0:T(4,128)} %broadcast_in_dim.119) | copy-start | bytes 82948
  432.1 66.0 %copy-start.7 = (f32[3,2304]{1,0:T(4,128)S(1)}, f32[3,2304]{1,0:T(4,128)}, u32[]{:S(2)}) copy-start(f32[3,2304]{1,0:T(4,128)} %broadcast_in_dim.114) | copy-start | bytes 82948
  432.1 111.9 %copy-start.5 = (f32[768,768]{1,0:T(8,128)S(1)}, f32[768,768]{1,0:T(8,128)}, u32[]{:S(2)}) copy-start(f32[768,768]{1,0:T(8,128)} %get-tuple-element.37) | copy-start | bytes 7077892
  540.3 3.7 copy-start.3
  540.3 3.7 copy-start.12
  540.3 3.7 copy-start.13
  544.0 1.3 copy-start.10
  545.3 213.6 %copy-start.1 = (s32[2,2]{1,0:T(2,128)S(1)}, s32[2,2]{1,0:T(2,128)}, u32[]{:S(2)}) copy-start(s32[2,2]{1,0:T(2,128)} %param.13) | copy-start | bytes 52
Sparse Core Ops, SparseCore 0:
  10.9 62.9 all-gather.6
  76.8 52.8 all-gather.8
  132.6 69.7 all-gather.10
  205.2 78.1 all-gather.12
  322.5 101.2 reduce-scatter.8
  429.1 104.0 reduce-scatter.14
  538.7 106.0 reduce-scatter.10
  651.2 106.0 reduce-scatter.12
